TPU v7x, 32 devices: a whole 2x2x4 slice. The times are simulated.
32 devices in a mesh: group: 2 (over x), ep: 16 (over z, y, core).
Axes of the slice: x: 2, y: 2, z: 4, core: 2. Of those that a mesh axis runs over, the one named last changes fastest.
Arguments:
- query: bfloat16 [128, 4096], P(('group', 'ep')), parts along dimension 0, may hold values from -6 to 6
- fresh_key: bfloat16 [128, 256], P(('group', 'ep')), parts along dimension 0, may hold values from -6 to 6
- fresh_value: bfloat16 [128, 256], P(('group', 'ep')), parts along dimension 0, may hold values from -6 to 6
- stored_keys: bfloat16 [128, 512, 256], P(('group', 'ep')), parts along dimension 0, may hold values from -30 to 30
- stored_values: bfloat16 [128, 512, 256], P(('group', 'ep')), parts along dimension 0, may hold values from -6 to 6
- lengths: int32 [128], P(('group', 'ep')), parts along dimension 0, may hold values from 2 to 512, as said below
- q_gain: float32 [128], replicated, may hold values from 0.1 to 1.9
- key_norm_gain: float32 [128], replicated, may hold values from 0.1 to 1.9
- expert_input: bfloat16 [2048, 2048], P(('group', 'ep')), parts along dimension 0, may hold values from -6 to 6
- routing: int32 [2048, 8], P(('group', 'ep')), parts along dimension 0, may hold values from 0 to 15, all different within a row; in each aligned block of 64 rows (0 to 63, 64 to 127, ...) at most 64 rows name the same one
- gate_weights: float32 [2048, 8], P(('group', 'ep')), parts along dimension 0, may hold values from 0.05 to 1
- w_gate_up: bfloat16 [16, 2048, 1536], P('ep'), may hold values from -0.125 to 0.125
- w_down: bfloat16 [16, 768, 2048], P('ep'), may hold values from -0.21875 to 0.21875
Outputs:
- attention_out: bfloat16 [128, 4096], P(('group', 'ep')), parts along dimension 0
- expert_out: bfloat16 [2048, 2048], P(('group', 'ep')), parts along dimension 0
There are 2 independent parts, one for each index of `group`. A program takes and returns all parts, laid end to end along the dimension named above; an argument that names none is the same for every part. Nothing has to cross between parts.
Inputs may be any that keep to these rules, and one draw needn't show every extreme that they name: `routing`: each row names 8 different experts; among the rows of one device no expert is named more than 64 times, a bound that some block reaches. The new token stands at position lengths; some row has 512.
All inputs are finite; a program needn't handle non-finite values.
Results may differ from a plain program's by a relative error of at most 0.0063.
Values may be sent and summed in bfloat16 or wider, within the bound.
A program may use at most 64 MiB of HBM per device.

v0:
```python
import jax
import jax.numpy as jnp
from jax import lax
from jax.experimental import pallas as pl
from jax.experimental.pallas import tpu as pltpu
from jax.sharding import PartitionSpec as P

QUERY_HEADS = 32
KEY_VALUE_HEADS = 2
HEAD_SIZE = 128


def apply_rotation(all_values, positions):
    half = all_values.shape[-1] // 2
    steps = jnp.arange(half).astype(jnp.float32)
    inverse = jnp.exp(-2.0 * steps / all_values.shape[-1] * jnp.log(jnp.float32(1000000.0)))
    angles = positions.astype(jnp.float32)[:, None] * inverse[None, :]
    cosine = jnp.cos(angles)[:, None, :]
    sine = jnp.sin(angles)[:, None, :]
    first = all_values[..., :half]
    second = all_values[..., half:]
    return jnp.concatenate(
        [first * cosine - second * sine, second * cosine + first * sine], axis=-1
    )


def per_head_norm(all_values, gain):
    scale = lax.rsqrt(jnp.mean(all_values * all_values, axis=-1, keepdims=True) + 1e-06)
    return all_values * scale * gain


def attention(
    query, fresh_key, fresh_value, stored_keys, stored_values, lengths, q_gain, key_norm_gain
):
    token_count = query.shape[0]
    context_output = stored_keys.shape[1]
    query_groups = QUERY_HEADS // KEY_VALUE_HEADS
    normalized_query = apply_rotation(
        per_head_norm(
            query.astype(jnp.float32).reshape(token_count, QUERY_HEADS, HEAD_SIZE), q_gain
        ),
        lengths,
    ).astype(jnp.bfloat16)
    normalized_key = apply_rotation(
        per_head_norm(
            fresh_key.astype(jnp.float32).reshape(token_count, KEY_VALUE_HEADS, HEAD_SIZE),
            key_norm_gain,
        ),
        lengths,
    ).astype(jnp.bfloat16)
    grouped_queries = normalized_query.reshape(
        token_count, KEY_VALUE_HEADS, query_groups, HEAD_SIZE
    )
    all_keys = stored_keys.reshape(token_count, context_output, KEY_VALUE_HEADS, HEAD_SIZE)
    scores = jnp.einsum(
        "rhgd,rchd->rhgc", grouped_queries, all_keys, preferred_element_type=jnp.float32
    ) / jnp.sqrt(jnp.float32(HEAD_SIZE))
    own = jnp.sum(
        grouped_queries.astype(jnp.float32) * normalized_key.astype(jnp.float32)[:, :, None, :],
        axis=-1,
    ) / jnp.sqrt(jnp.float32(HEAD_SIZE))
    live = jnp.arange(context_output)[None, :] < lengths[:, None]
    scores = jnp.where(live[:, None, None, :], scores, -jnp.inf)
    top = jnp.maximum(jnp.max(scores, axis=-1), own)
    weights = jnp.exp(scores - top[..., None])
    own_weight = jnp.exp(own - top)
    total = jnp.sum(weights, axis=-1) + own_weight
    probs = (weights / total[..., None]).astype(jnp.bfloat16)
    fresh_token_prob = (own_weight / total).astype(jnp.bfloat16)
    all_values = stored_values.reshape(token_count, context_output, KEY_VALUE_HEADS, HEAD_SIZE)
    mixed_output = jnp.einsum(
        "rhgc,rchd->rhgd", probs, all_values, preferred_element_type=jnp.float32
    )
    mixed_output = mixed_output + fresh_token_prob.astype(jnp.float32)[
        ..., None
    ] * fresh_value.astype(jnp.float32).reshape(token_count, KEY_VALUE_HEADS, 1, HEAD_SIZE)
    return mixed_output.reshape(token_count, QUERY_HEADS * HEAD_SIZE).astype(jnp.bfloat16)


def feed_forward(slots, w_gate_up, w_down):
    layout = slots.shape
    flat = slots.reshape(-1, layout[-1])
    hidden_units = w_down.shape[1]
    both = jnp.dot(flat, w_gate_up[0], preferred_element_type=jnp.float32)
    hidden = (jax.nn.silu(both[:, :hidden_units]) * both[:, hidden_units:]).astype(jnp.bfloat16)
    answer = jnp.dot(hidden, w_down[0], preferred_element_type=jnp.float32).astype(jnp.bfloat16)
    return answer.reshape(layout)


LAYERS = 4
EXTRA = 128
Y_FIRST = 768
PIECE = 512
UP, DOWN, ACROSS, MATE = 0, 1, 2, 3


def expert_kernel(
    x_ref, routing_ref, gates_ref, up_hbm, down_hbm, out_ref,
    rows_all, sums, from_mate, from_across, from_layer, w_up, w_down, hidden,
    w_sem, ag_send, ag_recv, mate_send, mate_recv, across_send, across_recv, chain_send, chain_recv,
):
    me = lax.axis_index("ep")
    core, side, layer = lax.rem(me, 2), lax.rem(me // 2, 2), me // 4
    last = LAYERS - 1
    experts = LAYERS * 4
    count, width = x_ref.shape
    total = width + EXTRA
    hid = w_down.shape[0]
    mate, across = me + 1 - 2 * core, me + 2 - 4 * side
    has_up, has_down = layer < last, layer > 0
    edge = jnp.logical_or(layer == 0, layer == last)
    everyone = layer >= 0
    spans = (pl.ds(Y_FIRST, total - Y_FIRST), pl.ds(0, Y_FIRST))
    pending = []

    up_copy = pltpu.make_async_copy(up_hbm, w_up, w_sem.at[0])
    down_copy = pltpu.make_async_copy(down_hbm, w_down, w_sem.at[1])
    up_copy.start()
    down_copy.start()

    def block(l, s, c):
        return (l * 2 + s) * 2 + c

    def rows(b):
        return pl.ds(pl.multiple_of(b * count, count), count)

    def remote(src, dst, send, recv, target):
        return pltpu.make_async_remote_copy(
            src_ref=src, dst_ref=dst, send_sem=send, recv_sem=recv,
            device_id={"ep": target}, device_id_type=pl.DeviceIdType.MESH,
        )

    def gather(h, b, way):
        target = {UP: me + 4, DOWN: me - 4, ACROSS: across, MATE: mate}[way]
        part = rows_all.at[rows(b), spans[h]]
        return remote(part, part, ag_send.at[h, way, b], ag_recv.at[h, b], target)

    def send(cond, h, b, way):
        @pl.when(cond)
        def _():
            gather(h, b, way).start()

        pending.append((cond, lambda: gather(h, b, way).wait_send()))

    def arrived(h, b):
        gather(h, b, MATE).wait_recv()

    gates = gates_ref[...]
    share = gates / jnp.sum(gates, axis=1, keepdims=True)
    picks = routing_ref[...]
    lane = lax.broadcasted_iota(jnp.int32, (count, EXTRA), 1)
    expert = jnp.where(lane < experts, lane, lane - experts)
    spread = jnp.zeros((count, EXTRA), jnp.float32)
    for k in range(picks.shape[1]):
        spread = spread + jnp.where(picks[:, k : k + 1] == expert, share[:, k : k + 1], 0.0)
    high = spread.astype(jnp.bfloat16).astype(jnp.float32)
    extra = jnp.where(lane < experts, high, spread - high)
    rows_all[rows(me), pl.ds(0, width)] = x_ref[...]
    rows_all[rows(me), pl.ds(width, EXTRA)] = extra.astype(jnp.bfloat16)

    barrier = pltpu.get_barrier_semaphore()

    def hello(target):
        pl.semaphore_signal(
            barrier, inc=1, device_id={"ep": target}, device_id_type=pl.DeviceIdType.MESH
        )

    hello(mate)
    hello(across)
    pl.when(has_up)(lambda: hello(me + 4))
    pl.when(has_down)(lambda: hello(me - 4))
    pl.semaphore_wait(barrier, jnp.where(edge, 3, 4))

    for h in (1, 0):
        send(everyone, h, me, ACROSS)
        send(has_up, h, me, UP)
        send(has_down, h, me, DOWN)
        send(everyone, h, me, MATE)
    arrived(1, across)
    send(has_up, 1, across, UP)
    send(has_down, 1, across, DOWN)
    send(everyone, 1, across, MATE)

    def forward(distance):
        for step, onward, way in ((-distance, has_up, UP), (distance, has_down, DOWN)):
            other = layer + step
            present = other >= 0 if step < 0 else other <= last
            both = jnp.logical_and(present, onward)
            for h, s in ((1, side), (1, 1 - side), (0, side)):
                b = block(other, s, core)
                pl.when(present)(lambda h=h, b=b: arrived(h, b))
                send(both, h, b, way)
                if h == 0:
                    send(present, h, b, ACROSS)
                send(present, h, b, MATE)

    def order(step):
        first = (0, 1, 2, 3)[step]
        second = (1, 0, 2, 3)[step]
        near = jnp.where(edge, first, second)
        return jnp.where(layer < 2, near, last - near)

    def mlp(now):
        where = pl.ds(pl.multiple_of(now * 4 * count, 4 * count), 4 * count)
        wide = 256

        @pl.loop(0, hid // wide)
        def _(j):
            at = pl.multiple_of(j * wide, wide)
            x = rows_all[where, pl.ds(0, width)]
            gate = jnp.dot(x, w_up[:, pl.ds(at, wide)], preferred_element_type=jnp.float32)
            up = jnp.dot(
                x, w_up[:, pl.ds(pl.multiple_of(hid + at, wide), wide)],
                preferred_element_type=jnp.float32,
            )
            hidden[:, pl.ds(at, wide)] = (jax.nn.silu(gate) * up).astype(jnp.bfloat16)

        shares = rows_all[where, pl.ds(width, EXTRA)].astype(jnp.float32)
        lanes = lax.broadcasted_iota(jnp.int32, shares.shape, 1)
        mine = jnp.logical_or(lanes == me, lanes == me + experts)
        weight = jnp.sum(jnp.where(mine, shares, 0.0), axis=1, keepdims=True)

        @pl.loop(0, width // wide)
        def _(j):
            at = pl.ds(pl.multiple_of(j * wide, wide), wide)
            answer = jnp.dot(hidden[...], w_down[:, at], preferred_element_type=jnp.float32)
            answer = answer.astype(jnp.bfloat16).astype(jnp.float32)
            sums[where, at] = (weight * answer).astype(jnp.bfloat16)

    def piece(p):
        return pl.ds(pl.multiple_of(p * PIECE, PIECE), PIECE)

    pieces = width // PIECE

    def to_mate(now, s):
        slot = now * 2 + s
        return remote(
            sums.at[rows(block(now, s, 1 - core))], from_mate.at[rows(slot)],
            mate_send.at[slot], mate_recv.at[slot], mate,
        )

    def to_across(now, p):
        return remote(
            sums.at[rows(block(now, 1 - side, core)), piece(p)], from_across.at[rows(now), piece(p)],
            across_send.at[now, p], across_recv.at[now, p], across,
        )

    def to_layer(now, p):
        upward = now > layer
        slot = jnp.where(jnp.logical_and(now < layer, now == layer - 1), LAYERS, now)
        return remote(
            sums.at[rows(block(now, side, core)), piece(p)], from_layer.at[rows(slot), piece(p)],
            chain_send.at[now, p], chain_recv.at[slot, p], jnp.where(upward, me + 4, me - 4),
        )

    def chain_arrived(slot, p):
        part = from_layer.at[rows(slot), piece(p)]
        remote(part, part, chain_send.at[0, p], chain_recv.at[slot, p], mate).wait_recv()

    def wide32(ref, *index):
        return ref[index].astype(jnp.float32)

    def pair(now):
        to_mate(now, 1 - side).wait_recv()

        @pl.loop(0, pieces)
        def _(p):
            b, slot = block(now, 1 - side, core), now * 2 + 1 - side
            value = wide32(sums, rows(b), piece(p)) + wide32(from_mate, rows(slot), piece(p))
            sums[rows(b), piece(p)] = value.astype(jnp.bfloat16)
            to_across(now, p).start()

        to_mate(now, side).wait_recv()

    def held(now, p):
        to_across(now, p).wait_recv()
        b, slot = block(now, side, core), now * 2 + side
        value = wide32(sums, rows(b), piece(p)) + wide32(from_mate, rows(slot), piece(p))
        return value + wide32(from_across, rows(now), piece(p))

    def chain(now, incoming):
        @pl.loop(0, pieces)
        def _(p):
            value = held(now, p)
            if incoming:
                chain_arrived(now, p)
                value = value + wide32(from_layer, rows(now), piece(p))
            sums[rows(block(now, side, core)), piece(p)] = value.astype(jnp.bfloat16)
            to_layer(now, p).start()

    for step in range(LAYERS):
        now = order(step)
        if step > 0:
            forward(step)
        arrived(0, block(now, 1 - side, core))
        send(everyone, 0, block(now, 1 - side, core), MATE)
        for s in range(2):
            for h in range(2):
                arrived(h, block(now, s, 1 - core))
        if step == 0:
            up_copy.wait()
            down_copy.wait()
        mlp(now)
        to_mate(now, 1 - side).start()
        to_mate(now, side).start()
        pair(now)
        if step > 1:
            pl.when(edge)(lambda step=step: chain(order(step - 1), False))

    @pl.when(edge)
    def _():
        chain(order(3), False)

    @pl.when(jnp.logical_not(edge))
    def _():
        for step in (2, 3, 1):
            chain(order(step), True)

    @pl.loop(0, pieces)
    def _(p):
        value = held(layer, p)
        pl.when(has_down)(lambda: chain_arrived(layer, p))
        pl.when(has_up)(lambda: chain_arrived(LAYERS, p))
        below = wide32(from_layer, rows(layer), piece(p))
        above = wide32(from_layer, rows(LAYERS), piece(p))
        value = value + jnp.where(has_down, below, 0.0) + jnp.where(has_up, above, 0.0)
        out_ref[:, piece(p)] = value.astype(jnp.bfloat16)

    for cond, wait in pending:
        pl.when(cond)(wait)
    for step in range(LAYERS):
        now = order(step)
        to_mate(now, 0).wait_send()
        to_mate(now, 1).wait_send()

        @pl.loop(0, pieces)
        def _(p):
            to_across(now, p).wait_send()
            if step > 0:
                to_layer(now, p).wait_send()


def grid_experts(expert_input, routing, gate_weights, w_gate_up, w_down):
    count, width = expert_input.shape
    devices = LAYERS * 4
    pieces = width // PIECE
    dma = pltpu.SemaphoreType.DMA
    vmem, anywhere = pl.BlockSpec(memory_space=pltpu.VMEM), pl.BlockSpec(memory_space=pl.ANY)
    return pl.pallas_call(
        expert_kernel,
        out_shape=jax.ShapeDtypeStruct((count, width), jnp.bfloat16),
        in_specs=[vmem, vmem, vmem, anywhere, anywhere],
        out_specs=vmem,
        scratch_shapes=[
            pltpu.VMEM((devices * count, width + EXTRA), jnp.bfloat16),
            pltpu.VMEM((devices * count, width), jnp.bfloat16),
            pltpu.VMEM((LAYERS * 2 * count, width), jnp.bfloat16),
            pltpu.VMEM((LAYERS * count, width), jnp.bfloat16),
            pltpu.VMEM(((LAYERS + 1) * count, width), jnp.bfloat16),
            pltpu.VMEM(w_gate_up.shape, jnp.bfloat16),
            pltpu.VMEM(w_down.shape, jnp.bfloat16),
            pltpu.VMEM((4 * count, w_down.shape[0]), jnp.bfloat16),
            dma((2,)),
            dma((2, 4, devices)),
            dma((2, devices)),
            dma((LAYERS * 2,)),
            dma((LAYERS * 2,)),
            dma((LAYERS, pieces)),
            dma((LAYERS, pieces)),
            dma((LAYERS, pieces)),
            dma((LAYERS + 1, pieces)),
        ],
        compiler_params=pltpu.CompilerParams(
            collective_id=0, has_side_effects=True, vmem_limit_bytes=44 * 1024 * 1024
        ),
        name="expert_grid",
    )(expert_input, routing, gate_weights, w_gate_up, w_down)


def local(
    query,
    fresh_key,
    fresh_value,
    stored_keys,
    stored_values,
    lengths,
    q_gain,
    key_norm_gain,
    expert_input,
    routing,
    gate_weights,
    w_gate_up,
    w_down,
):
    attention_out = attention(
        query, fresh_key, fresh_value, stored_keys, stored_values, lengths, q_gain, key_norm_gain
    )
    devices = lax.axis_size("ep")
    if devices == LAYERS * 4:
        expert_out = grid_experts(expert_input, routing, gate_weights, w_gate_up[0], w_down[0])
        return (attention_out, expert_out)
    experts_all = devices * w_gate_up.shape[0]
    rows, width = expert_input.shape
    picks = routing.shape[1]
    capacity = 2 * rows * picks // experts_all
    share = gate_weights / jnp.sum(gate_weights, axis=1, keepdims=True)
    flat_ids = routing.reshape(-1)
    onehot = (flat_ids[:, None] == jnp.arange(experts_all)[None, :]).astype(jnp.int32)
    earlier = jnp.sum((jnp.cumsum(onehot, axis=0) - onehot) * onehot, axis=1)
    slot = flat_ids * capacity + earlier
    padded = jnp.concatenate([expert_input, jnp.zeros((1, width), jnp.bfloat16)], axis=0)
    sources = jnp.arange(rows * picks) // picks
    table = jnp.full((experts_all * capacity,), rows, jnp.int32).at[slot].set(sources)
    outgoing = padded[table].reshape(experts_all, capacity, width)
    arrived = lax.all_to_all(outgoing, "ep", split_axis=0, concat_axis=0, tiled=True)
    results = feed_forward(arrived, w_gate_up, w_down)
    returned = lax.all_to_all(results, "ep", split_axis=0, concat_axis=0, tiled=True)
    picked = returned.reshape(experts_all * capacity, width)[slot].reshape(rows, picks, width)
    mixed_output = jnp.zeros((rows, width), jnp.float32)
    for column in range(picks):
        mixed_output = mixed_output + share[:, column : column + 1] * picked[:, column].astype(
            jnp.float32
        )
    return (attention_out, mixed_output.astype(jnp.bfloat16))


def solution(mesh):
    return jax.shard_map(
        local,
        mesh=mesh,
        in_specs=(
            P(("group", "ep"), None),
            P(("group", "ep"), None),
            P(("group", "ep"), None),
            P(("group", "ep"), None, None),
            P(("group", "ep"), None, None),
            P(("group", "ep")),
            P(),
            P(),
            P(("group", "ep"), None),
            P(("group", "ep"), None),
            P(("group", "ep"), None),
            P("ep", None, None),
            P("ep", None, None),
        ),
        out_specs=(P(("group", "ep"), None), P(("group", "ep"), None)),
        check_vma=False,
    )
```

profile of v0, /device:TPU:0, one launch (start us, length us, event | category | flops | bytes accessed | tf_op | source)
XLA Modules:
  0.0 111.9 jit_solution(10110662708744798233)
XLA Ops:
  0.6 0.8 reshape.166
  1.4 0.1 multiply_reduce_fusion.1
  1.5 0.7 multiply_multiply_fusion
  2.3 0.7 convert_element_type.55
  2.9 0.1 multiply_cosine_fusion
  3.1 0.1 maximum_convert_fusion
  3.2 0.8 convert_bitcast_fusion
  4.0 0.1 fusion.9
  4.1 0.7 fusion.10
  4.8 0.1 subtract_convert_fusion
  4.9 0.2 multiply_reduce_fusion
  5.1 0.7 iota_compare_fusion
  5.8 0.5 fusion.14
  6.3 0.2 fusion.6
  6.6 0.7 reshape.167
  7.3 1.5 %fusion.1 = bf16[4,2,16,128]{3,2,1,0:T(8,128)(2,1)S(1)} fusion(f32[4,2,16,512]{3,2,1,0:T(8,128)S(1)} %get-tuple-element.11, f32[4,2,16]{2,1,0:T(2,128)S(1)} %get-tuple-element.5, f32[4,2,16]{2,1,0:T(2,128)S(1)} %multiply_maximum_fusion, f32[4,2,128]{2,1,0:T(2,128)S(1)} %reshape.167, f32[4,2,16]{2,1,0:T(2,128)S(1)} %get-tuple-element.4, ...), kind=kOutput, calls=%fused_computation.3 | convolution fusion | flops 17022976 | bytes 1349120 | tf_op jit(solution)/shard_map/rhgc,rchd->rhgd/dot_general | solution.py:71
  8.8 0.6 copy.36
  9.5 0.8 copy.17.routing_ref
  10.2 0.8 copy.18.gates_ref
  11.0 2.8 %copy-done.1 = bf16[1,2048,1536]{2,1,0:T(8,128)(2,1)S(1)} copy-done((bf16[1,2048,1536]{2,1,0:T(8,128)(2,1)S(1)}, bf16[1,2048,1536]{2,1,0:T(8,128)(2,1)}, u32[]{:S(2)}) %copy-start.1) | copy-done | bytes 6291480
  13.8 1.9 %copy-done.2 = bf16[1,768,2048]{2,1,0:T(8,128)(2,1)S(1)} copy-done((bf16[1,768,2048]{2,1,0:T(8,128)(2,1)S(1)}, bf16[1,768,2048]{2,1,0:T(8,128)(2,1)}, u32[]{:S(2)}) %copy-start.2) | copy-done | bytes 3145752
  15.7 0.9 copy-done.3
  16.6 94.6 %expert_grid.1 = bf16[64,2048]{1,0:T(8,128)(2,1)S(1)} custom-call(bf16[64,2048]{1,0:T(8,128)(2,1)S(1)} %copy-done.3, s32[64,8]{1,0:T(8,128)S(1)} %copy.17.routing_ref, f32[64,8]{1,0:T(8,128)S(1)} %copy.18.gates_ref, bf16[2048,1536]{1,0:T(8,128)(2,1)S(1)} %bitcast.34, bf16[768,2048]{1,0:T(8,128)(2,1)S(1)} %bitcast.35), custom_call_target="tpu_custom_call" | custom-call | tf_op jit(solution)/shard_map/expert_grid/pallas_call | solution.py:349
  111.2 0.7 copy.38
  (11 shorter events, 0.1 us)
Async XLA Ops:
  0.6 5.2 %copy-start = (bf16[4,512,256]{2,1,0:T(8,128)(2,1)S(1)}, bf16[4,512,256]{2,1,0:T(8,128)(2,1)}, u32[]{:S(2)}) copy-start(bf16[4,512,256]{2,1,0:T(8,128)(2,1)} %param.16) | copy-start | bytes 3145732
  11.0 2.8 %copy-start.1 = (bf16[1,2048,1536]{2,1,0:T(8,128)(2,1)S(1)}, bf16[1,2048,1536]{2,1,0:T(8,128)(2,1)}, u32[]{:S(2)}) copy-start(bf16[1,2048,1536]{2,1,0:T(8,128)(2,1)} %param.24) | copy-start | bytes 18874372
  13.8 1.9 %copy-start.2 = (bf16[1,768,2048]{2,1,0:T(8,128)(2,1)S(1)}, bf16[1,768,2048]{2,1,0:T(8,128)(2,1)}, u32[]{:S(2)}) copy-start(bf16[1,768,2048]{2,1,0:T(8,128)(2,1)} %param.25) | copy-start | bytes 9437188
  15.7 0.9 copy-start.3
where the time goes:
time: 112 us
  Pallas kernels  94.6 us (84%)
  local copies, waits for them, and re-layouts  9.99 us (9%)
  other arithmetic  4.61 us (4%)
  matrix products  2.03 us (2%)
    pallas_call x1, Pallas kernels, grid_experts(): pl.pallas_call(expert_kernel, out_shape=jax.ShapeDtypeStruct((count, widt...  94.6 us
    unnamed x12, local copies, waits for them, and re-layouts  8.52 us

commit v1 on v0

--- a/solution.py
+++ b/solution.py
@@ -94,8 +94,73 @@
 UP, DOWN, ACROSS, MATE = 0, 1, 2, 3
 
 
+def attend(
+    q_ref, key_ref, value_ref, lengths_ref, q_gain_ref, key_gain_ref, keys, values, queries_at,
+    mixed_at, out_ref,
+):
+    half = HEAD_SIZE // 2
+    queries = q_ref.shape[1] // HEAD_SIZE
+    queries_each = queries // KEY_VALUE_HEADS
+    lane = lax.broadcasted_iota(jnp.int32, (1, HEAD_SIZE), 1)
+    steps = jnp.where(lane < half, lane, lane - half).astype(jnp.float32)
+    inverse = jnp.exp(-2.0 * steps / HEAD_SIZE * jnp.log(jnp.full(steps.shape, 1000000.0)))
+    token = lax.broadcasted_iota(jnp.int32, (keys.shape[0], 1), 0)
+    lengths = jnp.zeros(token.shape, jnp.int32)
+    for r in range(keys.shape[0]):
+        lengths = jnp.where(token == r, lengths_ref[r], lengths)
+    angles = lengths.astype(jnp.float32) * inverse
+    cosine = jnp.cos(angles)
+    sine = jnp.where(lane < half, -jnp.sin(angles), jnp.sin(angles))
+    fresh_keys = key_ref[...].astype(jnp.float32)
+    fresh_values = value_ref[...].astype(jnp.float32)
+    root = jnp.sqrt(jnp.full((1, 1), float(HEAD_SIZE)))
+
+    def turned(v, gain):
+        scale = lax.rsqrt(jnp.mean(v * v, axis=-1, keepdims=True) + 1e-06)
+        v = v * scale * gain
+        swapped = jnp.concatenate([v[:, half:], v[:, :half]], axis=-1)
+        return (v * cosine + swapped * sine).astype(jnp.bfloat16).astype(jnp.float32)
+
+    for h in range(queries):
+        at = slice(h * HEAD_SIZE, (h + 1) * HEAD_SIZE)
+        v = turned(q_ref[:, at].astype(jnp.float32), q_gain_ref[...])
+        for r in range(keys.shape[0]):
+            queries_at[r * queries + h : r * queries + h + 1, :] = v[r : r + 1]
+    fresh_turned = [
+        turned(fresh_keys[:, h * HEAD_SIZE : (h + 1) * HEAD_SIZE], key_gain_ref[...])
+        for h in range(KEY_VALUE_HEADS)
+    ]
+
+    for r in range(keys.shape[0]):
+        for h in range(KEY_VALUE_HEADS):
+            columns = slice(h * HEAD_SIZE, (h + 1) * HEAD_SIZE)
+            start = r * queries + h * queries_each
+            mine = queries_at[start : start + queries_each, :].astype(jnp.bfloat16)
+            scores = lax.dot_general(
+                mine, keys[r, :, columns], (((1,), (1,)), ((), ())),
+                preferred_element_type=jnp.float32,
+            ) / root
+            own = jnp.sum(mine.astype(jnp.float32) * fresh_turned[h][r : r + 1], axis=-1, keepdims=True) / root
+            position = lax.broadcasted_iota(jnp.int32, scores.shape, 1)
+            scores = jnp.where(position < lengths_ref[r], scores, -jnp.inf)
+            top = jnp.maximum(jnp.max(scores, axis=-1, keepdims=True), own)
+            weights = jnp.exp(scores - top)
+            own_weight = jnp.exp(own - top)
+            total = jnp.sum(weights, axis=-1, keepdims=True) + own_weight
+            probs = (weights / total).astype(jnp.bfloat16)
+            own_prob = (own_weight / total).astype(jnp.bfloat16).astype(jnp.float32)
+            mixed = jnp.dot(probs, values[r, :, columns], preferred_element_type=jnp.float32)
+            mixed = mixed + own_prob * fresh_values[r : r + 1, columns]
+            for g in range(queries_each):
+                at = (h * queries_each + g) * HEAD_SIZE
+                mixed_at[r : r + 1, at : at + HEAD_SIZE] = mixed[g : g + 1]
+    out_ref[...] = mixed_at[...].astype(jnp.bfloat16)
+
+
 def expert_kernel(
-    x_ref, routing_ref, gates_ref, up_hbm, down_hbm, out_ref,
+    x_ref, routing_ref, gates_ref, q_ref, key_ref, value_ref, lengths_ref, q_gain_ref, key_gain_ref,
+    keys_hbm, values_hbm, up_hbm, down_hbm, out_ref, attended_ref, keys, values, queries_at,
+    mixed_at,
     rows_all, sums, from_mate, from_across, from_layer, w_up, w_down, hidden,
     w_sem, ag_send, ag_recv, mate_send, mate_recv, across_send, across_recv, chain_send, chain_recv,
 ):
@@ -115,6 +180,10 @@
 
     up_copy = pltpu.make_async_copy(up_hbm, w_up, w_sem.at[0])
     down_copy = pltpu.make_async_copy(down_hbm, w_down, w_sem.at[1])
+    keys_copy = pltpu.make_async_copy(keys_hbm, keys, w_sem.at[2])
+    values_copy = pltpu.make_async_copy(values_hbm, values, w_sem.at[3])
+    keys_copy.start()
+    values_copy.start()
     up_copy.start()
     down_copy.start()
 
@@ -146,15 +215,15 @@
         gather(h, b, MATE).wait_recv()
 
     gates = gates_ref[...]
-    share = gates / jnp.sum(gates, axis=1, keepdims=True)
+    share = gates / jnp.sum(gates, axis=0, keepdims=True)
     picks = routing_ref[...]
-    lane = lax.broadcasted_iota(jnp.int32, (count, EXTRA), 1)
-    expert = jnp.where(lane < experts, lane, lane - experts)
-    spread = jnp.zeros((count, EXTRA), jnp.float32)
-    for k in range(picks.shape[1]):
-        spread = spread + jnp.where(picks[:, k : k + 1] == expert, share[:, k : k + 1], 0.0)
+    place = lax.broadcasted_iota(jnp.int32, (EXTRA, count), 0)
+    expert = jnp.where(place < experts, place, place - experts)
+    spread = jnp.zeros((EXTRA, count), jnp.float32)
+    for k in range(picks.shape[0]):
+        spread = spread + jnp.where(picks[k : k + 1, :] == expert, share[k : k + 1, :], 0.0)
     high = spread.astype(jnp.bfloat16).astype(jnp.float32)
-    extra = jnp.where(lane < experts, high, spread - high)
+    extra = jnp.where(place < experts, high, spread - high).T
     rows_all[rows(me), pl.ds(0, width)] = x_ref[...]
     rows_all[rows(me), pl.ds(width, EXTRA)] = extra.astype(jnp.bfloat16)
 
@@ -180,6 +249,13 @@
     send(has_up, 1, across, UP)
     send(has_down, 1, across, DOWN)
     send(everyone, 1, across, MATE)
+
+    keys_copy.wait()
+    values_copy.wait()
+    attend(
+        q_ref, key_ref, value_ref, lengths_ref, q_gain_ref, key_gain_ref, keys, values, queries_at,
+        mixed_at, attended_ref,
+    )
 
     def forward(distance):
         for step, onward, way in ((-distance, has_up, UP), (distance, has_down, DOWN)):
@@ -340,18 +416,31 @@
                 to_layer(now, p).wait_send()
 
 
-def grid_experts(expert_input, routing, gate_weights, w_gate_up, w_down):
+def grid_step(
+    query, fresh_key, fresh_value, stored_keys, stored_values, lengths, q_gain, key_norm_gain,
+    expert_input, routing, gate_weights, w_gate_up, w_down,
+):
     count, width = expert_input.shape
     devices = LAYERS * 4
     pieces = width // PIECE
     dma = pltpu.SemaphoreType.DMA
     vmem, anywhere = pl.BlockSpec(memory_space=pltpu.VMEM), pl.BlockSpec(memory_space=pl.ANY)
-    return pl.pallas_call(
+    expert_out, attended = pl.pallas_call(
         expert_kernel,
-        out_shape=jax.ShapeDtypeStruct((count, width), jnp.bfloat16),
-        in_specs=[vmem, vmem, vmem, anywhere, anywhere],
-        out_specs=vmem,
+        out_shape=(
+            jax.ShapeDtypeStruct((count, width), jnp.bfloat16),
+            jax.ShapeDtypeStruct(query.shape, jnp.bfloat16),
+        ),
+        in_specs=[vmem] * 6
+        + [pl.BlockSpec(memory_space=pltpu.SMEM)]
+        + [vmem] * 2
+        + [anywhere] * 4,
+        out_specs=(vmem, vmem),
         scratch_shapes=[
+            pltpu.VMEM(stored_keys.shape, jnp.bfloat16),
+            pltpu.VMEM(stored_values.shape, jnp.bfloat16),
+            pltpu.VMEM((query.shape[0] * QUERY_HEADS, HEAD_SIZE), jnp.float32),
+            pltpu.VMEM(query.shape, jnp.float32),
             pltpu.VMEM((devices * count, width + EXTRA), jnp.bfloat16),
             pltpu.VMEM((devices * count, width), jnp.bfloat16),
             pltpu.VMEM((LAYERS * 2 * count, width), jnp.bfloat16),
@@ -360,7 +449,7 @@
             pltpu.VMEM(w_gate_up.shape, jnp.bfloat16),
             pltpu.VMEM(w_down.shape, jnp.bfloat16),
             pltpu.VMEM((4 * count, w_down.shape[0]), jnp.bfloat16),
-            dma((2,)),
+            dma((4,)),
             dma((2, 4, devices)),
             dma((2, devices)),
             dma((LAYERS * 2,)),
@@ -371,10 +460,15 @@
             dma((LAYERS + 1, pieces)),
         ],
         compiler_params=pltpu.CompilerParams(
-            collective_id=0, has_side_effects=True, vmem_limit_bytes=44 * 1024 * 1024
+            collective_id=0, has_side_effects=True, vmem_limit_bytes=58 * 1024 * 1024
         ),
         name="expert_grid",
-    )(expert_input, routing, gate_weights, w_gate_up, w_down)
+    )(
+        expert_input, routing.T, gate_weights.T, query, fresh_key, fresh_value,
+        lengths, q_gain[None, :], key_norm_gain[None, :],
+        stored_keys, stored_values, w_gate_up, w_down,
+    )
+    return (attended, expert_out)
 
 
 def local(
@@ -392,13 +486,15 @@
     w_gate_up,
     w_down,
 ):
+    devices = lax.axis_size("ep")
+    if devices == LAYERS * 4:
+        return grid_step(
+            query, fresh_key, fresh_value, stored_keys, stored_values, lengths, q_gain,
+            key_norm_gain, expert_input, routing, gate_weights, w_gate_up[0], w_down[0],
+        )
     attention_out = attention(
         query, fresh_key, fresh_value, stored_keys, stored_values, lengths, q_gain, key_norm_gain
     )
-    devices = lax.axis_size("ep")
-    if devices == LAYERS * 4:
-        expert_out = grid_experts(expert_input, routing, gate_weights, w_gate_up[0], w_down[0])
-        return (attention_out, expert_out)
     experts_all = devices * w_gate_up.shape[0]
     rows, width = expert_input.shape
     picks = routing.shape[1]

time: 112 us -> 99.7 us (0.89)
  local copies, waits for them, and re-layouts: 9.99 us -> 3.05 us
  other arithmetic: 4.61 us -> 0 us
  matrix products: 2.03 us -> 0 us
  Pallas kernels: 94.6 us -> 95.8 us
    unnamed x12 -> x2, local copies, waits for them, and re-layouts: 8.52 us -> 3.05 us
    dot_general x2 -> x0, matrix products: 2.03 us -> none  [the longest x1 1.53 us: attention(): jnp.einsum('rhgc,rchd->rhgd', probs, all_values, preferred_element_type=j...]
    mul x2 -> x0, other arithmetic: 1.47 us -> none  [per_head_norm(): return all_values * scale * gain]
    pallas_call x1, Pallas kernels: 94.6 us -> 95.8 us  [grid_step(): pl.pallas_call(expert_kernel, out_shape=(jax.ShapeDtypeStruct((count, wid...]
where the time goes in v1:
time: 99.7 us; the launch traced here: 99.4 us
  Pallas kernels  95.8 us (96%)
  local copies, waits for them, and re-layouts  3.05 us (3%)
    pallas_call x1, Pallas kernels, grid_step(): pl.pallas_call(expert_kernel, out_shape=(jax.ShapeDtypeStruct((count, wid...  95.8 us
    unnamed x2, local copies, waits for them, and re-layouts  3.05 us

profile of v1, /device:TPU:0, one launch (start us, length us, event | category | flops | bytes accessed | tf_op | source)
XLA Modules:
  0.0 99.4 jit_solution(973527759961440692)
XLA Ops:
  0.6 95.8 %expert_grid.1 = (bf16[64,2048]{1,0:T(8,128)(2,1)}, bf16[4,4096]{1,0:T(4,128)(2,1)}) custom-call(bf16[64,2048]{1,0:T(8,128)(2,1)} %x_ref.1, s32[8,64]{1,0:T(8,128)} %bitcast.8, f32[8,64]{1,0:T(8,128)} %bitcast.9, bf16[4,4096]{1,0:T(4,128)(2,1)} %q_ref.1, bf16[4,256]{1,0:T(4,128)(2,1)} %key_ref.1, bf16[4,256]{1,0:T(4,128)(2,1)} %value_ref.1, s32[4]{0:T(128)} %lengths_ref.1, ...), custom_call_target="tpu_custom_call" | custom-call | tf_op jit(solution)/shard_map/expert_grid/pallas_call | solution.py:428
  96.4 1.4 %copy.17 = bf16[4,4096]{1,0:T(4,128)(2,1)} copy(bf16[4,4096]{1,0:T(4,128)(2,1)} %get-tuple-element.8) | data formatting | bytes 65536
  97.8 1.7 %copy.18 = bf16[64,2048]{1,0:T(8,128)(2,1)} copy(bf16[64,2048]{1,0:T(8,128)(2,1)} %get-tuple-element.9) | data formatting | bytes 524288

commit v2 on v1

--- a/solution.py
+++ b/solution.py
@@ -366,8 +366,6 @@
 
     for step in range(LAYERS):
         now = order(step)
-        if step > 0:
-            forward(step)
         arrived(0, block(now, 1 - side, core))
         send(everyone, 0, block(now, 1 - side, core), MATE)
         for s in range(2):
@@ -379,6 +377,8 @@
         mlp(now)
         to_mate(now, 1 - side).start()
         to_mate(now, side).start()
+        if step < LAYERS - 1:
+            forward(step + 1)
         pair(now)
         if step > 1:
             pl.when(edge)(lambda step=step: chain(order(step - 1), False))

time: 99.7 us -> 83.9 us (0.84)
  Pallas kernels: 95.8 us -> 80 us
    pallas_call x1, Pallas kernels: 95.8 us -> 80 us  [grid_step(): pl.pallas_call(expert_kernel, out_shape=(jax.ShapeDtypeStruct((count, wid...]
where the time goes in v2:
time: 83.9 us; the launch traced here: 83.7 us
  Pallas kernels  80 us (95%)
  local copies, waits for them, and re-layouts  3.05 us (4%)
    pallas_call x1, Pallas kernels, grid_step(): pl.pallas_call(expert_kernel, out_shape=(jax.ShapeDtypeStruct((count, wid...  80 us
    unnamed x2, local copies, waits for them, and re-layouts  3.05 us

profile of v2, /device:TPU:0, one launch (start us, length us, event | category | flops | bytes accessed | tf_op | source)
XLA Modules:
  0.0 83.7 jit_solution(16142134598840804276)
XLA Ops:
  0.6 80.0 %expert_grid.1 = (bf16[64,2048]{1,0:T(8,128)(2,1)}, bf16[4,4096]{1,0:T(4,128)(2,1)}) custom-call(bf16[64,2048]{1,0:T(8,128)(2,1)} %x_ref.1, s32[8,64]{1,0:T(8,128)} %bitcast.8, f32[8,64]{1,0:T(8,128)} %bitcast.9, bf16[4,4096]{1,0:T(4,128)(2,1)} %q_ref.1, bf16[4,256]{1,0:T(4,128)(2,1)} %key_ref.1, bf16[4,256]{1,0:T(4,128)(2,1)} %value_ref.1, s32[4]{0:T(128)} %lengths_ref.1, ...), custom_call_target="tpu_custom_call" | custom-call | tf_op jit(solution)/shard_map/expert_grid/pallas_call | solution.py:428
  80.7 1.4 %copy.17 = bf16[4,4096]{1,0:T(4,128)(2,1)} copy(bf16[4,4096]{1,0:T(4,128)(2,1)} %get-tuple-element.8) | data formatting | bytes 65536
  82.0 1.7 %copy.18 = bf16[64,2048]{1,0:T(8,128)(2,1)} copy(bf16[64,2048]{1,0:T(8,128)(2,1)} %get-tuple-element.9) | data formatting | bytes 524288
